TPU v7x, 32 devices: a whole 2x2x4 slice. The times are simulated.
32 devices in a mesh: orient: 8 (over z, x), frame: 4 (over y, core).
Axes of the slice: x: 2, y: 2, z: 4, core: 2. Of those that a mesh axis runs over, the one named last changes fastest.
Arguments:
- volume: float32 [507904], P('orient'), may hold values from 0.1 to 10
- voxel_index: int32 [16, 1024], P(None, 'orient'), may hold values from 0 to 63487
- pixel_index: int32 [16, 1024], P('orient'), may hold values from 0 to 4095
- weights: bfloat16 [16, 1024], P('orient'), may hold values from 0.049804688 to 0.5
- background: float32 [4096], replicated, may hold values from 0.2 to 1
- counts: int32 [1024, 4096], P('frame'), may hold values from 0 to 16, as said below
Outputs:
- new_volume: float32 [507904], P('orient')
- probs: float32 [16, 1024], P('orient', 'frame')
Inputs may be any that keep to these rules, and one draw needn't show every extreme that they name: Photon counts; frames differ in their mean count.
All inputs are finite; a program needn't handle non-finite values.
Results may differ from a plain program's by a relative error of at most 0.0003.
Values sent between devices are 32-bit elements; how exact they have to be, the bound alone decides.
A program may use at most 64 MiB of HBM per device.

v0:
```python
import jax
import jax.numpy as jnp
from jax import lax
from jax.sharding import PartitionSpec as P

prior_weight = 0.05


def on_device(volume, voxel_index, pixel_index, weights, background, counts):
    ori_local = pixel_index.shape[0]
    pixels = background.shape[0]
    wfloat = weights.astype(jnp.float32)
    row_ids = jnp.arange(ori_local, dtype=jnp.int32)[:, None]
    gathered = volume[voxel_index]
    received = lax.all_to_all(gathered, "orient", split_axis=0, concat_axis=1, tiled=True)
    contrib = wfloat * received
    slices = (
        jnp.zeros((ori_local, pixels), jnp.float32).at[row_ids, pixel_index].add(contrib)
        + background[None, :]
    )
    counts_f = counts.astype(jnp.float32)
    loglike = lax.dot_general(
        jnp.log(slices),
        counts_f,
        (((1,), (1,)), ((), ())),
        precision=lax.Precision.HIGHEST,
        preferred_element_type=jnp.float32,
    )
    loglike = loglike - jnp.sum(slices, axis=1)[:, None]
    score = 64.0 / pixels * loglike
    local_top = jnp.max(score, axis=0)
    global_top = lax.pmax(local_top, "orient")
    expo_terms = jnp.exp(score - global_top[None, :])
    global_total = lax.psum(jnp.sum(expo_terms, axis=0), "orient")
    probs = expo_terms / global_total[None, :]
    numerator = jnp.dot(
        probs, counts_f, precision=lax.Precision.HIGHEST, preferred_element_type=jnp.float32
    )
    denominator = jnp.sum(probs, axis=1)
    summed_num, summed_den = lax.psum((numerator, denominator), "frame")
    picked = jnp.take_along_axis(summed_num, pixel_index, axis=1)
    entry_num = wfloat * picked
    entry_den = wfloat * summed_den[:, None]
    back_num, back_den = (
        lax.all_to_all(entry_num, "orient", split_axis=1, concat_axis=0, tiled=True),
        lax.all_to_all(entry_den, "orient", split_axis=1, concat_axis=0, tiled=True),
    )
    acc_num = jnp.zeros(volume.shape, jnp.float32).at[voxel_index].add(back_num)
    acc_den = jnp.zeros(volume.shape, jnp.float32).at[voxel_index].add(back_den)
    new_volume = (acc_num + prior_weight * volume) / (acc_den + prior_weight)
    return (new_volume, probs)


def solution(mesh):
    in_specs = (
        P("orient"),
        P(None, "orient"),
        P("orient", None),
        P("orient", None),
        P(),
        P("frame", None),
    )
    out_specs = (P("orient"), P("orient", "frame"))
    return jax.shard_map(
        on_device, mesh=mesh, in_specs=in_specs, out_specs=out_specs, check_vma=False
    )
```

profile of v0, /device:TPU:0, one launch (start us, length us, event | category | flops | bytes accessed | tf_op | source)
XLA Modules:
  0.0 158.8 jit_solution(17978657418144633096)
XLA Ops:
  0.6 0.0 copy-start
  0.6 0.7 broadcast_clamp_fusion
  1.4 0.0 copy-start.2
  1.4 0.0 copy-start.7
  1.4 0.0 copy-start.6
  1.4 0.0 copy-start.4
  1.4 19.9 %gather_fusion = f32[2048]{0:T(1024)} fusion(f32[63488]{0:T(1024)} %param.6, s32[2048]{0:T(1024)S(1)} %broadcast_clamp_fusion), kind=kCustom, calls=%fused_computation | custom fusion | bytes 24576 | tf_op jit(solution)/shard_map/gather | solution.py:14
  21.2 7.3 %all-to-all-start = ((f32[8,2,128]{2,1,0:T(2,128)}), f32[8,2,128]{2,1,0:T(2,128)S(1)}, u32[]{:S(2)}, u32[]{:S(2)}) async-start(f32[8,2,128]{2,1,0:T(2,128)} %bitcast.2), calls=%async_computation | async-start | bytes 16384 | tf_op jit(solution)/shard_map/all_to_all | solution.py:15
  28.5 0.0 copy-done
  28.5 0.0 copy-done.2
  28.6 0.0 copy-done.7
  28.6 0.1 and_reduce_fusion
  28.7 0.0 copy-done.6
  28.7 0.1 multiply_reduce_fusion
  28.8 6.2 %all-to-all-done = f32[8,2,128]{2,1,0:T(2,128)S(1)} async-done(((f32[8,2,128]{2,1,0:T(2,128)}), f32[8,2,128]{2,1,0:T(2,128)S(1)}, u32[]{:S(2)}, u32[]{:S(2)}) %all-to-all-start) | async-done | bytes 8224 | tf_op jit(solution)/shard_map/all_to_all | solution.py:15
  35.0 0.0 copy-done.4
  35.0 11.6 %scatter_fusion.1 = f32[8192]{0:T(1024)S(1)} fusion(f32[8192]{0:T(1024)S(1)} %bitcast.43, s32[2048]{0:T(1024)S(1)} %bitcast.46, f32[2048]{0:T(1024)S(1)} %bitcast.47), kind=kCustom, calls=%fused_computation.4 | custom fusion | flops 2048 | bytes 32768
  46.6 0.2 reduce_sum.27
  46.8 5.6 %fusion.22 = (f32[256]{0:T(256)S(1)}, f32[2,256]{1,0:T(2,128)S(1)}) fusion(f32[2]{0:T(128)S(1)} %reduce_sum.27, s32[256,4096]{1,0:T(8,128)} %param.11, f32[2,4096]{1,0:T(2,128)S(1)} %reshape.33), kind=kOutput, calls=%fused_computation.40 | convolution fusion | flops 26215680 | bytes 4230152 | tf_op jit(solution)/shard_map/dot_general | solution.py:22
  52.3 17.7 %pmax.7 = f32[256]{0:T(256)S(1)} all-reduce(f32[256]{0:T(256)S(1)} %get-tuple-element.8), channel_id=1, replica_groups=mesh['orient'=8,'frame'=4] {'orient'}, use_global_device_ids=true, to_apply=%region_3.0 | all-reduce | flops 256 | bytes 2048 | tf_op jit(solution)/shard_map/pmax | solution.py:32
  70.1 18.6 %psum.21 = f32[256]{0:T(256)S(1)} all-reduce(f32[256]{0:T(256)S(1)} %fusion.19), channel_id=1, replica_groups=mesh['orient'=8,'frame'=4] {'orient'}, use_global_device_ids=true, to_apply=%region_5.0 | all-reduce | flops 256 | bytes 2048 | tf_op jit(solution)/shard_map/psum | solution.py:34
  88.6 0.1 fusion.20
  88.8 0.0 copy-start.5
  88.8 4.3 %fusion = f32[2,4096]{1,0:T(2,128)S(1)} fusion(f32[2,256]{1,0:T(2,128)S(1)} %get-tuple-element.5, s32[256,4096]{1,0:T(8,128)} %param.11), kind=kOutput, calls=%fused_computation.5 | convolution fusion | flops 26214400 | bytes 4229120 | tf_op jit(solution)/shard_map/dot_general | solution.py:36
  93.1 10.5 %all-reduce = (f32[2,4096]{1,0:T(2,128)S(1)}, f32[2]{0:T(128)S(1)}) all-reduce(f32[2,4096]{1,0:T(2,128)S(1)} %fusion, f32[2]{0:T(128)S(1)} %get-tuple-element.4), channel_id=1, replica_groups=mesh['orient'=8,'frame'=4] {'frame'}, use_global_device_ids=true, to_apply=%region_6.0 | all-reduce | flops 8194 | bytes 65552 | tf_op jit(solution)/shard_map/psum | solution.py:40
  103.6 0.0 copy-start.1
  103.6 0.0 copy-start.3
  103.6 17.7 %gather_fusion.1 = f32[2048]{0:T(1024)S(1)} fusion(f32[2,4096]{1,0:T(2,128)S(1)} %get-tuple-element.2, s32[2048]{0:T(1024)S(1)} %bitcast.44), kind=kCustom, calls=%fused_computation.1 | custom fusion | bytes 32768 | tf_op jit(solution)/shard_map/jit(take_along_axis)/gather | solution.py:41
  121.3 0.0 copy-done.5
  121.3 0.7 fusion.15
  122.0 3.3 %all-to-all-start.1 = ((f32[2,8,128]{2,0,1:T(2,128)}), f32[2,8,128]{2,0,1:T(2,128)S(1)}, u32[]{:S(2)}, u32[]{:S(2)}) async-start(f32[2,8,128]{2,0,1:T(2,128)} %get-tuple-element.7), calls=%async_computation.1 | async-start | bytes 16384 | tf_op jit(solution)/shard_map/all_to_all | solution.py:45
  125.3 0.0 copy-done.1
  125.4 6.4 %all-to-all-done.1 = f32[2,8,128]{2,0,1:T(2,128)S(1)} async-done(((f32[2,8,128]{2,0,1:T(2,128)}), f32[2,8,128]{2,0,1:T(2,128)S(1)}, u32[]{:S(2)}, u32[]{:S(2)}) %all-to-all-start.1) | async-done | bytes 8224 | tf_op jit(solution)/shard_map/all_to_all | solution.py:45
  131.8 3.3 %all-to-all-start.2 = ((f32[2,8,128]{2,0,1:T(2,128)}), f32[2,8,128]{2,0,1:T(2,128)S(1)}, u32[]{:S(2)}, u32[]{:S(2)}) async-start(f32[2,8,128]{2,0,1:T(2,128)} %get-tuple-element.6), calls=%async_computation.2 | async-start | bytes 16384 | tf_op jit(solution)/shard_map/all_to_all | solution.py:46
  135.1 0.0 copy-done.3
  135.2 11.6 %scatter_fusion = f32[63488]{0:T(1024)S(1)} fusion(f32[63488]{0:T(1024)S(1)} %broadcast_multiply_fusion, s32[2048]{0:T(1024)S(1)} %fusion.16, f32[2048]{0:T(1024)S(1)} %bitcast.45), kind=kCustom, calls=%fused_computation.2 | custom fusion | flops 2048 | bytes 32768 | tf_op jit(solution)/shard_map/scatter-add | solution.py:48
  146.8 0.0 all-to-all-done.2
  146.8 11.3 %scatter_custom_fusion.1 = f32[63488]{0:T(1024)S(1)} fusion(s32[2048]{0:T(1024)S(1)} %fusion.16, f32[2048]{0:T(1024)S(1)} %bitcast.48, f32[]{:T(128)} %constant.9.clone.1), kind=kCustom, calls=%fused_computation.11 | custom fusion | flops 2048 | bytes 253956 | tf_op jit(solution)/shard_map/scatter-add | solution.py:49
  158.1 0.7 div.13
  (15 shorter events, 0.2 us)
Async XLA Ops:
  0.6 27.9 %copy-start = (f32[4096]{0:T(1024)S(1)}, f32[4096]{0:T(1024)}, u32[]{:S(2)}) copy-start(f32[4096]{0:T(1024)} %param.10) | copy-start | bytes 49156
  1.4 27.2 %copy-start.2 = (s32[2,1024]{1,0:T(2,128)S(1)}, s32[2,1024]{1,0:T(2,128)}, u32[]{:S(2)}) copy-start(s32[2,1024]{1,0:T(2,128)} %param.8) | copy-start | bytes 24580
  1.4 27.2 %copy-start.7 = (s32[2]{0:T(128)S(1)}, s32[2]{0:T(128)}, u32[]{:S(2)}) copy-start(s32[2]{0:T(128)} %constant.39) | copy-start | bytes 28
  1.4 27.3 %copy-start.6 = (s32[2]{0:T(128)S(1)}, s32[2]{0:T(128)}, u32[]{:S(2)}) copy-start(s32[2]{0:T(128)} %constant.36) | copy-start | bytes 28
  1.4 33.7 %copy-start.4 = (bf16[2,1024]{1,0:T(2,128)(2,1)S(1)}, bf16[2,1024]{1,0:T(2,128)(2,1)}, u32[]{:S(2)}) copy-start(bf16[2,1024]{1,0:T(2,128)(2,1)} %param.9) | copy-start | bytes 12292
  21.2 13.8 %all-to-all-start = ((f32[8,2,128]{2,1,0:T(2,128)}), f32[8,2,128]{2,1,0:T(2,128)S(1)}, u32[]{:S(2)}, u32[]{:S(2)}) async-start(f32[8,2,128]{2,1,0:T(2,128)} %bitcast.2), calls=%async_computation | async-start | bytes 16384 | tf_op jit(solution)/shard_map/all_to_all | solution.py:15
  88.8 32.6 %copy-start.5 = (f32[2,256]{1,0:T(2,128)}, f32[2,256]{1,0:T(2,128)S(1)}, u32[]{:S(2)}) copy-start(f32[2,256]{1,0:T(2,128)S(1)} %get-tuple-element.5) | copy-start | bytes 6148
  103.6 21.8 %copy-start.1 = (f32[63488]{0:T(1024)S(1)}, f32[63488]{0:T(1024)}, u32[]{:S(2)}) copy-start(f32[63488]{0:T(1024)} %param.6) | copy-start | bytes 761860
  103.6 31.6 %copy-start.3 = (s32[16,128]{1,0:T(8,128)S(1)}, s32[16,128]{1,0:T(8,128)}, u32[]{:S(2)}) copy-start(s32[16,128]{1,0:T(8,128)} %param.7) | copy-start | bytes 24580
  122.0 9.8 %all-to-all-start.1 = ((f32[2,8,128]{2,0,1:T(2,128)}), f32[2,8,128]{2,0,1:T(2,128)S(1)}, u32[]{:S(2)}, u32[]{:S(2)}) async-start(f32[2,8,128]{2,0,1:T(2,128)} %get-tuple-element.7), calls=%async_computation.1 | async-start | bytes 16384 | tf_op jit(solution)/shard_map/all_to_all | solution.py:45
  131.8 15.0 %all-to-all-start.2 = ((f32[2,8,128]{2,0,1:T(2,128)}), f32[2,8,128]{2,0,1:T(2,128)S(1)}, u32[]{:S(2)}, u32[]{:S(2)}) async-start(f32[2,8,128]{2,0,1:T(2,128)} %get-tuple-element.6), calls=%async_computation.2 | async-start | bytes 16384 | tf_op jit(solution)/shard_map/all_to_all | solution.py:46
where the time goes:
time: 159 us
  blocking collectives  46.7 us (29%)
  local copies, waits for them, and re-layouts  37.7 us (24%)
  other arithmetic  37.1 us (23%)
  starting transfers between devices  13.9 us (9%)
  waiting for transfers between devices  12.6 us (8%)
  matrix products  9.9 us (6%)
    gather x1, local copies, waits for them, and re-layouts, on_device(): gathered = volume[voxel_index]  19.9 us
    psum x1, blocking collectives, on_device(): global_total = lax.psum(jnp.sum(expo_terms, axis=0), 'orient')  18.6 us
    pmax x1, blocking collectives, on_device(): global_top = lax.pmax(local_top, 'orient')  17.7 us
    gather x2, local copies, waits for them, and re-layouts, on_device(): picked = jnp.take_along_axis(summed_num, pixel_index, axis=1)  17.7 us
    unnamed x6, other arithmetic  11.8 us
    scatter-add x1, other arithmetic, on_device(): acc_num = jnp.zeros(volume.shape, jnp.float32).at[voxel_index].add(back_num)  11.6 us
    scatter-add x1, other arithmetic, on_device(): acc_den = jnp.zeros(volume.shape, jnp.float32).at[voxel_index].add(back_den)  11.3 us
    psum x1, blocking collectives, on_device(): summed_num, summed_den = lax.psum((numerator, denominator), 'frame')  10.5 us
  transfers between devices with their start and end apart: 3, of which 2 were waited for; matrix products, arithmetic and copies ran while one was open for 7% of the time, Pallas kernels for 0%

commit v1 on v0

v1 whole, which is shorter than its diff:
```python
import functools

import jax
import jax.numpy as jnp
from jax import lax
from jax.experimental import pallas as pl
from jax.experimental.pallas import tpu as pltpu
from jax.sharding import PartitionSpec as P

prior_weight = 0.05
LANES = 128
GROUP = 16
CHUNKS = 4
MESH = pl.DeviceIdType.MESH
F32, BF16, I32 = jnp.float32, jnp.bfloat16, jnp.int32


def each(count, body):
    if count <= 16:
        for i in range(count):
            body(i)
    else:
        lax.fori_loop(0, count, lambda i, _: (body(i), 0)[1], 0)


def at(i, size):
    return pl.ds(i * size if isinstance(i, int) else pl.multiple_of(i * size, size), size)


def parts(x, count):
    out = []
    for _ in range(count):
        p = x.astype(BF16).astype(F32)
        out.append(p)
        x = x - p
    return out


def dot_nt(a, b):
    return lax.dot_general(a, b, (((1,), (1,)), ((), ())), preferred_element_type=F32)


def lane_pick(rows, lane):
    return jnp.take_along_axis(rows, lane, axis=1, mode="promise_in_bounds")


def kernel(
    n, m,
    vol_ref, vidx_ref, pix_ref, w_ref, bg_ref, cnt_ref,
    newv_ref, probs_ref,
    cnt_i, cnt_b, vals, got_vals, pw, got_pw, pix_hot, spread, logs, scores, all_scores,
    pix_mine, w_mine, row_hot, col_val, sums, acc_scr,
    cnt_sem, val_send, val_recv, pw_send, pw_recv, sc_send, sc_recv, sum_send, sum_recv,
):
    me = lax.axis_index("orient")
    fr = lax.axis_index("frame")
    local = pix_ref.shape[0]
    total = n * local
    frames, pixels = cnt_ref.shape
    pix_rows = pixels // LANES
    vox_rows = vol_ref.shape[0]
    step = frames // CHUNKS
    per_group = GROUP // local

    barrier = pltpu.get_barrier_semaphore()

    def greet_o(d):
        pl.semaphore_signal(barrier, inc=1, device_id={"orient": lax.rem(me + d + 1, n)}, device_id_type=MESH)

    def greet_f(d):
        pl.semaphore_signal(barrier, inc=1, device_id={"frame": lax.rem(fr + d + 1, m)}, device_id_type=MESH)

    each(n - 1, greet_o)
    each(m - 1, greet_f)

    loads = [
        pltpu.make_async_copy(
            cnt_ref.at[pl.ds(i * step, step)], cnt_i.at[pl.ds(i * step, step)], cnt_sem.at[i]
        )
        for i in range(CHUNKS)
    ]
    for c in loads:
        c.start()

    def gather_group(g):
        idx = vidx_ref[at(g, GROUP), :]
        row = lax.shift_right_logical(idx, 7)
        lane = lax.bitwise_and(idx, LANES - 1)

        def body(t, acc):
            base = pl.multiple_of(t * 8, 8)
            block = vol_ref[pl.ds(base, 8), :]
            for i in range(8):
                line = jnp.broadcast_to(block[i : i + 1, :], (GROUP, LANES))
                acc = jnp.where(row == base + i, lane_pick(line, lane), acc)
            return acc

        acc = lax.fori_loop(0, vox_rows // 8, body, jnp.zeros((GROUP, LANES), F32), unroll=2)
        for j in range(per_group):
            vals[g * per_group + j] = acc[j * local : (j + 1) * local, :]

    each(total // GROUP, gather_group)

    def fill_pw(j):
        pw[j, 0:local] = pix_ref[:, at(j, LANES)].astype(F32)
        pw[j, local : 2 * local] = w_ref[:, at(j, LANES)].astype(F32)

    each(n, fill_pw)

    pl.semaphore_wait(barrier, n + m - 2)

    def val_copy(d):
        to = lax.rem(me + d + 1, n)
        return pltpu.make_async_remote_copy(
            src_ref=vals.at[to], dst_ref=got_vals.at[me],
            send_sem=val_send.at[d], recv_sem=val_recv.at[me],
            device_id={"orient": to}, device_id_type=MESH,
        )

    def pw_copy(d):
        to = lax.rem(me + d + 1, n)
        return pltpu.make_async_remote_copy(
            src_ref=pw.at[to], dst_ref=got_pw.at[me],
            send_sem=pw_send.at[d], recv_sem=pw_recv.at[me],
            device_id={"orient": to}, device_id_type=MESH,
        )

    def score_copy(d):
        to = lax.rem(me + d + 1, n)
        return pltpu.make_async_remote_copy(
            src_ref=scores, dst_ref=all_scores.at[me],
            send_sem=sc_send.at[d], recv_sem=sc_recv.at[me],
            device_id={"orient": to}, device_id_type=MESH,
        )

    def sum_copy(d):
        to = lax.rem(fr + d + 1, m)
        return pltpu.make_async_remote_copy(
            src_ref=sums.at[fr], dst_ref=sums.at[fr],
            send_sem=sum_send.at[d], recv_sem=sum_recv.at[fr],
            device_id={"frame": to}, device_id_type=MESH,
        )

    def arrivals(buffer, sems, own, count, send_sems):
        def body(d):
            src = lax.rem(own + d + 1, count)
            pltpu.make_async_remote_copy(
                src_ref=buffer.at[src], dst_ref=buffer.at[src],
                send_sem=send_sems.at[d], recv_sem=sems.at[src],
                device_id={"orient": me}, device_id_type=MESH,
            ).wait_recv()

        each(count - 1, body)

    each(n - 1, lambda d: val_copy(d).start())
    each(n - 1, lambda d: pw_copy(d).start())
    got_vals[me] = vals[me]
    got_pw[me] = pw[me]

    def hot_pix(s):
        for o in range(local):
            lane = lax.bitwise_and(pix_ref[pl.ds(o, 1), at(s, LANES)], LANES - 1)
            hot = lax.broadcasted_iota(I32, (LANES, LANES), 0) == lane
            pix_hot[o, :, at(s, LANES)] = jnp.where(hot, 1.0, 0.0).astype(BF16)

    each(n, hot_pix)

    for i in range(CHUNKS):
        loads[i].wait()

        def cast(t, _, i=i):
            rows = pl.ds(pl.multiple_of(i * step + t * 16, 16), 16)
            cnt_b[rows, :] = cnt_i[rows, :].astype(F32).astype(BF16)
            return 0

        lax.fori_loop(0, step // 16, cast, 0)

    arrivals(got_vals, val_recv, me, n, val_send)

    def spread_slab(s):
        contrib = got_vals[s] * pw[s, local : 2 * local]
        for o in range(local):
            row = lax.shift_right_logical(pix_ref[pl.ds(o, 1), at(s, LANES)], 7)
            hit = lax.broadcasted_iota(I32, (pix_rows, LANES), 0) == row
            for k, part in enumerate(parts(contrib[o : o + 1, :], 3)):
                spread[o, k * pix_rows : (k + 1) * pix_rows, at(s, LANES)] = jnp.where(hit, part, 0.0).astype(BF16)

    each(n, spread_slab)

    logs[...] = jnp.zeros_like(logs)
    slice_sums = []
    for o in range(local):
        d3 = dot_nt(spread[o], pix_hot[o])
        sl = d3[0:pix_rows] + d3[pix_rows : 2 * pix_rows] + d3[2 * pix_rows : 3 * pix_rows] + bg_ref[...]
        slice_sums.append(jnp.sum(jnp.sum(sl, axis=1, keepdims=True), axis=0, keepdims=True))
        lg = jnp.log(sl)
        for r in range(pix_rows):
            logs[o : o + 1, r * LANES : (r + 1) * LANES] = lg[r : r + 1, :]
    pad = logs.shape[0]
    lv = logs[...]
    stack = jnp.concatenate(parts(lv, 3) + [jnp.zeros_like(lv)], axis=0).astype(BF16)
    ll = dot_nt(stack, cnt_b[...])
    ll = ll[0:pad] + ll[pad : 2 * pad] + ll[2 * pad : 3 * pad]
    scores[...] = (64.0 / pixels) * (ll[0:local] - jnp.concatenate(slice_sums, axis=0))
    each(n - 1, lambda d: score_copy(d).start())
    all_scores[me] = scores[...]

    arrivals(got_pw, pw_recv, me, n, pw_send)

    def unpack(g):
        for j in range(per_group):
            src = got_pw[g * per_group + j]
            pix_mine[g, j * local : (j + 1) * local] = src[0:local].astype(I32)
            w_mine[g, j * local : (j + 1) * local] = src[local : 2 * local]

    each(total // GROUP, unpack)

    def hot_rows(g):
        idx = vidx_ref[at(g, GROUP), :]
        for o in range(GROUP):
            row = lax.shift_right_logical(idx[o : o + 1, :], 7)
            hit = lax.broadcasted_iota(I32, (vox_rows, LANES), 0) == row
            row_hot[:, o * LANES : (o + 1) * LANES] = jnp.where(hit, 1.0, 0.0).astype(BF16)

    hot_rows(0)

    arrivals(all_scores, sc_recv, me, n, sc_send)
    top = jnp.max(jnp.max(all_scores[...], axis=0), axis=0, keepdims=True)
    whole_sum = jnp.sum(jnp.sum(jnp.exp(all_scores[...] - top[None]), axis=0), axis=0, keepdims=True)
    probs_ref[...] = jnp.exp(scores[...] - top) / whole_sum

    def numerators(g):
        pieces = [
            jnp.exp(all_scores[g * per_group + j] - top) / whole_sum for j in range(per_group)
        ]
        pr = jnp.concatenate(pieces, axis=0)
        den = jnp.sum(pr, axis=1, keepdims=True)
        two = jnp.concatenate(parts(pr, 2), axis=0).astype(BF16)
        pix = pix_mine[g]
        row = lax.shift_right_logical(pix, 7)
        lane = lax.bitwise_and(pix, LANES - 1)
        acc = jnp.zeros((GROUP, LANES), F32)
        wide = 4
        for q in range(pix_rows // wide):
            d2 = jnp.dot(
                two, cnt_b[:, q * wide * LANES : (q + 1) * wide * LANES], preferred_element_type=F32
            )
            num = d2[0:GROUP] + d2[GROUP : 2 * GROUP]
            for i in range(wide):
                got = lane_pick(num[:, i * LANES : (i + 1) * LANES], lane)
                acc = jnp.where(row == q * wide + i, got, acc)
        sums[fr, 0, g] = acc
        sums[fr, 1, g] = jnp.broadcast_to(den, (GROUP, LANES))

    each(total // GROUP, numerators)
    each(m - 1, lambda d: sum_copy(d).start())

    def sum_arrivals(d):
        src = lax.rem(fr + d + 1, m)
        pltpu.make_async_remote_copy(
            src_ref=sums.at[src], dst_ref=sums.at[src],
            send_sem=sum_send.at[d], recv_sem=sum_recv.at[src],
            device_id={"frame": fr}, device_id_type=MESH,
        ).wait_recv()

    each(m - 1, sum_arrivals)

    def scatter(g):
        num, den = sums[0, 0, g], sums[0, 1, g]
        for f in range(1, m):
            num = num + sums[f, 0, g]
            den = den + sums[f, 1, g]
        wf = w_mine[g]
        four = parts(num * wf, 2) + parts(den * wf, 2)
        idx = vidx_ref[at(g, GROUP), :]
        lane = lax.bitwise_and(idx, LANES - 1)
        for o in range(GROUP):
            hit = lax.broadcasted_iota(I32, (LANES, LANES), 0) == lane[o : o + 1, :]
            for k in range(4):
                col_val[k * LANES : (k + 1) * LANES, o * LANES : (o + 1) * LANES] = jnp.where(
                    hit, four[k][o : o + 1, :], 0.0
                ).astype(BF16)
        return dot_nt(row_hot[...], col_val[...])

    def finish(acc):
        num = acc[:, 0:LANES] + acc[:, LANES : 2 * LANES]
        den = acc[:, 2 * LANES : 3 * LANES] + acc[:, 3 * LANES : 4 * LANES]
        newv_ref[...] = (num + prior_weight * vol_ref[...]) / (den + prior_weight)

    if total == GROUP:
        finish(scatter(0))
    else:
        acc_scr[...] = scatter(0)

        def more(g, _):
            hot_rows(g)
            acc_scr[...] += scatter(g)
            return 0

        lax.fori_loop(1, total // GROUP, more, 0)
        finish(acc_scr[...])

    each(n - 1, lambda d: val_copy(d).wait_send())
    each(n - 1, lambda d: pw_copy(d).wait_send())
    each(n - 1, lambda d: score_copy(d).wait_send())
    each(m - 1, lambda d: sum_copy(d).wait_send())


def on_device(n, m, volume, voxel_index, pixel_index, weights, background, counts):
    local, columns = pixel_index.shape
    total, entries = voxel_index.shape
    frames, pixels = counts.shape
    pix_rows = pixels // LANES
    vox_rows = volume.shape[0] // LANES
    groups = total // GROUP
    vmem = pl.BlockSpec(memory_space=pltpu.VMEM)
    dma = pltpu.SemaphoreType.DMA
    new_volume, probs = pl.pallas_call(
        functools.partial(kernel, n, m),
        out_shape=(
            jax.ShapeDtypeStruct((vox_rows, LANES), F32),
            jax.ShapeDtypeStruct((local, frames), F32),
        ),
        in_specs=[vmem] * 5 + [pl.BlockSpec(memory_space=pl.ANY)],
        out_specs=(vmem, vmem),
        scratch_shapes=[
            pltpu.VMEM((frames, pixels), I32),
            pltpu.VMEM((frames, pixels), BF16),
            pltpu.VMEM((n, local, LANES), F32),
            pltpu.VMEM((n, local, LANES), F32),
            pltpu.VMEM((n, 2 * local, LANES), F32),
            pltpu.VMEM((n, 2 * local, LANES), F32),
            pltpu.VMEM((local, LANES, columns), BF16),
            pltpu.VMEM((local, 3 * pix_rows, columns), BF16),
            pltpu.VMEM((8, pixels), F32),
            pltpu.VMEM((local, frames), F32),
            pltpu.VMEM((n, local, frames), F32),
            pltpu.VMEM((groups, GROUP, LANES), I32),
            pltpu.VMEM((groups, GROUP, LANES), F32),
            pltpu.VMEM((vox_rows, GROUP * LANES), BF16),
            pltpu.VMEM((4 * LANES, GROUP * LANES), BF16),
            pltpu.VMEM((m, 2, groups, GROUP, LANES), F32),
            pltpu.VMEM((vox_rows if groups > 1 else 8, 4 * LANES), F32),
            dma((CHUNKS,)),
            dma((n,)), dma((n,)), dma((n,)), dma((n,)), dma((n,)), dma((n,)),
            dma((m,)), dma((m,)),
        ],
        compiler_params=pltpu.CompilerParams(
            collective_id=0, has_side_effects=True, vmem_limit_bytes=44 * 1024 * 1024
        ),
    )(
        volume.reshape(vox_rows, LANES), voxel_index, pixel_index, weights,
        background.reshape(pix_rows, LANES), counts,
    )
    return (new_volume.reshape(-1), probs)


def solution(mesh):
    n, m = mesh.shape["orient"], mesh.shape["frame"]
    in_specs = (
        P("orient"),
        P(None, "orient"),
        P("orient", None),
        P("orient", None),
        P(),
        P("frame", None),
    )
    out_specs = (P("orient"), P("orient", "frame"))
    return jax.shard_map(
        functools.partial(on_device, n, m), mesh=mesh, in_specs=in_specs, out_specs=out_specs, check_vma=False
    )
```

time: 159 us -> 29.9 us (0.19)
  blocking collectives: 46.7 us -> 0 us
  other arithmetic: 37.1 us -> 0 us
  local copies, waits for them, and re-layouts: 37.7 us -> 7.21 us
  Pallas kernels: 0 us -> 21.7 us
  starting transfers between devices: 13.9 us -> 0 us
  waiting for transfers between devices: 12.6 us -> 0 us
  matrix products: 9.9 us -> 0 us
    gather x3 -> x0, local copies, waits for them, and re-layouts: 37.6 us -> none  [the longest x1 19.9 us: on_device(): gathered = volume[voxel_index]]
    psum x2 -> x0, blocking collectives: 29 us -> none  [the longest x1 18.6 us: on_device(): global_total = lax.psum(jnp.sum(expo_terms, axis=0), 'orient')]
    scatter-add x2 -> x0, other arithmetic: 22.9 us -> none  [the longest x1 11.6 us: on_device(): acc_num = jnp.zeros(volume.shape, jnp.float32).at[voxel_index].add(back_num)]
    pallas_call x0 -> x1, Pallas kernels: none -> 21.7 us  [on_device(): pl.pallas_call(functools.partial(kernel, n, m), out_shape=(jax.ShapeDtype...]
    pmax x1 -> x0, blocking collectives: 17.7 us -> none  [on_device(): global_top = lax.pmax(local_top, 'orient')]
    all_to_all x3 -> x0, starting transfers between devices: 13.9 us -> none  [the longest x1 7.25 us: on_device(): lax.all_to_all(gathered, 'orient', split_axis=0, concat_axis=1, tiled=True)]
    all_to_all x3 -> x0, waiting for transfers between devices: 12.6 us -> none  [the longest x1 6.41 us: on_device(): lax.all_to_all(entry_num, 'orient', split_axis=1, concat_axis=0, tiled=True)]
    unnamed x6 -> x0, other arithmetic: 11.8 us -> none
  transfers between devices with their start and end apart: 3 -> 0, of which waited for: 2 -> 0; matrix products, arithmetic and copies ran while one was open for 7% -> 0% of each run, Pallas kernels for 0% -> 0%
where the time goes in v1:
time: 29.9 us; the launch traced here: 29.6 us
  Pallas kernels  21.7 us (73%)
  local copies, waits for them, and re-layouts  7.21 us (24%)
  between operations  0.65 us (2%)
    pallas_call x1, Pallas kernels, on_device(): pl.pallas_call(functools.partial(kernel, n, m), out_shape=(jax.ShapeDtype...  21.7 us
    unnamed x14, local copies, waits for them, and re-layouts  7.21 us

profile of v1, /device:TPU:0, one launch (start us, length us, event | category | flops | bytes accessed | tf_op | source)
XLA Modules:
  0.0 29.6 jit_solution(10706909075784502211)
XLA Ops:
  0.6 0.0 copy-start
  0.6 2.2 %copy-done = s32[256,4096]{1,0:T(8,128)S(1)} copy-done((s32[256,4096]{1,0:T(8,128)S(1)}, s32[256,4096]{1,0:T(8,128)}, u32[]{:S(2)}) %copy-start) | copy-done | bytes 4194328
  2.8 0.0 copy-start.1
  2.8 0.9 %copy-done.1 = f32[63488]{0:T(1024)S(1)} copy-done((f32[63488]{0:T(1024)S(1)}, f32[63488]{0:T(1024)}, u32[]{:S(2)}) %copy-start.1) | copy-done | bytes 253976
  3.8 0.0 copy-start.2
  3.8 0.7 %copy-done.2 = f32[4096]{0:T(1024)S(1)} copy-done((f32[4096]{0:T(1024)S(1)}, f32[4096]{0:T(1024)}, u32[]{:S(2)}) %copy-start.2) | copy-done | bytes 16408
  4.5 0.0 copy-start.3
  4.5 0.7 %copy-done.3 = s32[16,128]{1,0:T(8,128)S(1)} copy-done((s32[16,128]{1,0:T(8,128)S(1)}, s32[16,128]{1,0:T(8,128)}, u32[]{:S(2)}) %copy-start.3) | copy-done | bytes 8216
  5.2 0.0 copy-start.4
  5.2 0.7 %copy-done.4 = s32[2,1024]{1,0:T(2,128)S(1)} copy-done((s32[2,1024]{1,0:T(2,128)S(1)}, s32[2,1024]{1,0:T(2,128)}, u32[]{:S(2)}) %copy-start.4) | copy-done | bytes 8216
  5.9 0.0 copy-start.5
  5.9 0.7 %copy-done.5 = bf16[2,1024]{1,0:T(2,128)(2,1)S(1)} copy-done((bf16[2,1024]{1,0:T(2,128)(2,1)S(1)}, bf16[2,1024]{1,0:T(2,128)(2,1)}, u32[]{:S(2)}) %copy-start.5) | copy-done | bytes 4120
  6.6 21.7 %shard_map.77 = (f32[496,128]{1,0:T(8,128)S(1)}, f32[2,256]{1,0:T(2,128)S(1)}) custom-call(f32[496,128]{1,0:T(8,128)S(1)} %bitcast.3, s32[16,128]{1,0:T(8,128)S(1)} %copy-done.3, s32[2,1024]{1,0:T(2,128)S(1)} %copy-done.4, bf16[2,1024]{1,0:T(2,128)(2,1)S(1)} %copy-done.5, f32[32,128]{1,0:T(8,128)S(1)} %bitcast.5, s32[256,4096]{1,0:T(8,128)S(1)} %copy-done), custom_call_target="tpu_custom_call" | custom-call | tf_op jit(solution)/shard_map/pallas_call | solution.py:318
  28.3 0.7 %copy.10 = f32[63488]{0:T(1024)} copy(f32[63488]{0:T(1024)S(1)} %bitcast.4) | data formatting | bytes 507904
  29.0 0.6 %copy.11 = f32[2,256]{1,0:T(2,128)} copy(f32[2,256]{1,0:T(2,128)S(1)} %get-tuple-element.9) | data formatting | bytes 4096
Async XLA Ops:
  0.6 2.2 %copy-start = (s32[256,4096]{1,0:T(8,128)S(1)}, s32[256,4096]{1,0:T(8,128)}, u32[]{:S(2)}) copy-start(s32[256,4096]{1,0:T(8,128)} %cnt_ref.1) | copy-start | bytes 12582916
  2.8 0.9 %copy-start.1 = (f32[63488]{0:T(1024)S(1)}, f32[63488]{0:T(1024)}, u32[]{:S(2)}) copy-start(f32[63488]{0:T(1024)} %param.6) | copy-start | bytes 761860
  3.8 0.7 %copy-start.2 = (f32[4096]{0:T(1024)S(1)}, f32[4096]{0:T(1024)}, u32[]{:S(2)}) copy-start(f32[4096]{0:T(1024)} %param.10) | copy-start | bytes 49156
  4.5 0.7 %copy-start.3 = (s32[16,128]{1,0:T(8,128)S(1)}, s32[16,128]{1,0:T(8,128)}, u32[]{:S(2)}) copy-start(s32[16,128]{1,0:T(8,128)} %vidx_ref.1) | copy-start | bytes 24580
  5.2 0.7 %copy-start.4 = (s32[2,1024]{1,0:T(2,128)S(1)}, s32[2,1024]{1,0:T(2,128)}, u32[]{:S(2)}) copy-start(s32[2,1024]{1,0:T(2,128)} %pix_ref.1) | copy-start | bytes 24580
  5.9 0.7 %copy-start.5 = (bf16[2,1024]{1,0:T(2,128)(2,1)S(1)}, bf16[2,1024]{1,0:T(2,128)(2,1)}, u32[]{:S(2)}) copy-start(bf16[2,1024]{1,0:T(2,128)(2,1)} %w_ref.1) | copy-start | bytes 12292

commit v2 on v1

--- a/solution.py
+++ b/solution.py
@@ -9,6 +9,8 @@
 
 prior_weight = 0.05
 LANES = 128
+VMEM_ALL = 64 * 1024 * 1024
+LEFT = 256 * 1024
 GROUP = 16
 CHUNKS = 4
 MESH = pl.DeviceIdType.MESH
@@ -46,15 +48,16 @@
 
 def kernel(
     n, m,
-    vol_ref, vidx_ref, pix_ref, w_ref, bg_ref, cnt_ref,
+    vol_hbm, vidx_hbm, pix_hbm, w_hbm, bg_hbm, cnt_ref,
     newv_ref, probs_ref,
+    vol_ref, vidx_ref, pix_ref, w_ref, bg_ref,
     cnt_i, cnt_b, vals, got_vals, pw, got_pw, pix_hot, spread, logs, scores, all_scores,
     pix_mine, w_mine, row_hot, col_val, sums, acc_scr,
-    cnt_sem, val_send, val_recv, pw_send, pw_recv, sc_send, sc_recv, sum_send, sum_recv,
+    in_sem, cnt_sem, val_send, val_recv, pw_send, pw_recv, sc_send, sc_recv, sum_send, sum_recv,
 ):
     me = lax.axis_index("orient")
     fr = lax.axis_index("frame")
-    local = pix_ref.shape[0]
+    local = pix_hbm.shape[0]
     total = n * local
     frames, pixels = cnt_ref.shape
     pix_rows = pixels // LANES
@@ -70,8 +73,19 @@
     def greet_f(d):
         pl.semaphore_signal(barrier, inc=1, device_id={"frame": lax.rem(fr + d + 1, m)}, device_id_type=MESH)
 
+    small = [
+        pltpu.make_async_copy(src, dst, in_sem.at[i])
+        for i, (src, dst) in enumerate(
+            [
+                (vidx_hbm, vidx_ref), (vol_hbm, vol_ref), (pix_hbm, pix_ref),
+                (w_hbm, w_ref), (bg_hbm, bg_ref),
+            ]
+        )
+    ]
     each(n - 1, greet_o)
     each(m - 1, greet_f)
+    for c in small:
+        c.start()
 
     loads = [
         pltpu.make_async_copy(
@@ -81,6 +95,8 @@
     ]
     for c in loads:
         c.start()
+    for c in small:
+        c.wait()
 
     def gather_group(g):
         idx = vidx_ref[at(g, GROUP), :]
@@ -306,6 +322,17 @@
     each(m - 1, lambda d: sum_copy(d).wait_send())
 
 
+def hand_out(vol_ref, probs_ref, vol_out, probs_out, sem):
+    copies = [
+        pltpu.make_async_copy(vol_ref, vol_out, sem.at[0]),
+        pltpu.make_async_copy(probs_ref, probs_out, sem.at[1]),
+    ]
+    for c in copies:
+        c.start()
+    for c in copies:
+        c.wait()
+
+
 def on_device(n, m, volume, voxel_index, pixel_index, weights, background, counts):
     local, columns = pixel_index.shape
     total, entries = voxel_index.shape
@@ -314,16 +341,22 @@
     vox_rows = volume.shape[0] // LANES
     groups = total // GROUP
     vmem = pl.BlockSpec(memory_space=pltpu.VMEM)
+    hbm = pl.BlockSpec(memory_space=pltpu.MemorySpace.HBM)
     dma = pltpu.SemaphoreType.DMA
     new_volume, probs = pl.pallas_call(
         functools.partial(kernel, n, m),
         out_shape=(
-            jax.ShapeDtypeStruct((vox_rows, LANES), F32),
-            jax.ShapeDtypeStruct((local, frames), F32),
+            pltpu.VMEM((vox_rows, LANES), F32),
+            pltpu.VMEM((local, frames), F32),
         ),
-        in_specs=[vmem] * 5 + [pl.BlockSpec(memory_space=pl.ANY)],
+        in_specs=[hbm] * 6,
         out_specs=(vmem, vmem),
         scratch_shapes=[
+            pltpu.VMEM((vox_rows, LANES), F32),
+            pltpu.VMEM((total, entries), I32),
+            pltpu.VMEM((local, columns), I32),
+            pltpu.VMEM((local, columns), BF16),
+            pltpu.VMEM((pix_rows, LANES), F32),
             pltpu.VMEM((frames, pixels), I32),
             pltpu.VMEM((frames, pixels), BF16),
             pltpu.VMEM((n, local, LANES), F32),
@@ -341,17 +374,27 @@
             pltpu.VMEM((4 * LANES, GROUP * LANES), BF16),
             pltpu.VMEM((m, 2, groups, GROUP, LANES), F32),
             pltpu.VMEM((vox_rows if groups > 1 else 8, 4 * LANES), F32),
-            dma((CHUNKS,)),
+            dma((5,)), dma((CHUNKS,)),
             dma((n,)), dma((n,)), dma((n,)), dma((n,)), dma((n,)), dma((n,)),
             dma((m,)), dma((m,)),
         ],
         compiler_params=pltpu.CompilerParams(
-            collective_id=0, has_side_effects=True, vmem_limit_bytes=44 * 1024 * 1024
+            collective_id=0, has_side_effects=True, vmem_limit_bytes=VMEM_ALL - 4 * (vox_rows * LANES + local * frames) - LEFT
         ),
     )(
         volume.reshape(vox_rows, LANES), voxel_index, pixel_index, weights,
         background.reshape(pix_rows, LANES), counts,
     )
+    new_volume, probs = pl.pallas_call(
+        hand_out,
+        out_shape=(
+            jax.ShapeDtypeStruct(new_volume.shape, F32),
+            jax.ShapeDtypeStruct(probs.shape, F32),
+        ),
+        in_specs=[vmem] * 2,
+        out_specs=[pl.BlockSpec(memory_space=pl.ANY)] * 2,
+        scratch_shapes=[dma((2,))],
+    )(new_volume, probs)
     return (new_volume.reshape(-1), probs)
 
 

time: 29.9 us -> 26.8 us (0.90)
  local copies, waits for them, and re-layouts: 7.21 us -> 1.26 us
  Pallas kernels: 21.7 us -> 24.6 us
    unnamed x14 -> x4, local copies, waits for them, and re-layouts: 7.21 us -> 1.26 us
    pallas_call x1 -> x2, Pallas kernels: 21.7 us -> 24.6 us  [the longest x1 23 us: on_device(): pl.pallas_call(functools.partial(kernel, n, m), out_shape=(pltpu.VMEM((vo...]
where the time goes in v2:
time: 26.8 us; the launch traced here: 26.6 us
  Pallas kernels  24.6 us (92%)
  local copies, waits for them, and re-layouts  1.26 us (5%)
  between operations  0.65 us (2%)
    pallas_call x1, Pallas kernels, on_device(): pl.pallas_call(functools.partial(kernel, n, m), out_shape=(pltpu.VMEM((vo...  23 us
    pallas_call x1, Pallas kernels, on_device(): pl.pallas_call(hand_out, out_shape=(jax.ShapeDtypeStruct(new_volume.shape...  1.66 us
    unnamed x4, local copies, waits for them, and re-layouts  1.26 us

profile of v2, /device:TPU:0, one launch (start us, length us, event | category | flops | bytes accessed | tf_op | source)
XLA Modules:
  0.0 26.6 jit_solution(1338457585883098843)
XLA Ops:
  0.6 23.0 %shard_map.77 = (f32[496,128]{1,0:T(8,128)S(1)}, f32[2,256]{1,0:T(2,128)S(1)}) custom-call(f32[496,128]{1,0:T(8,128)} %bitcast.3, s32[16,128]{1,0:T(8,128)} %vidx_hbm.1, s32[2,1024]{1,0:T(2,128)} %pix_hbm.1, bf16[2,1024]{1,0:T(2,128)(2,1)} %w_hbm.1, f32[32,128]{1,0:T(8,128)} %bitcast.4, s32[256,4096]{1,0:T(8,128)} %cnt_ref.1), custom_call_target="tpu_custom_call" | custom-call | tf_op jit(solution)/shard_map/pallas_call | solution.py:346
  23.6 0.0 copy-start
  23.6 0.7 %copy-done = f32[496,128]{1,0:T(8,128)} copy-done((f32[496,128]{1,0:T(8,128)}, f32[496,128]{1,0:T(8,128)S(1)}, u32[]{:S(2)}) %copy-start) | copy-done | bytes 253976
  24.3 0.0 copy-start.1
  24.3 0.6 %copy-done.1 = f32[2,256]{1,0:T(2,128)} copy-done((f32[2,256]{1,0:T(2,128)}, f32[2,256]{1,0:T(2,128)S(1)}, u32[]{:S(2)}) %copy-start.1) | copy-done | bytes 2072
  24.9 1.7 %shard_map.78 = (f32[496,128]{1,0:T(8,128)}, f32[2,256]{1,0:T(2,128)}) custom-call(f32[496,128]{1,0:T(8,128)} %copy-done, f32[2,256]{1,0:T(2,128)} %copy-done.1), custom_call_target="tpu_custom_call" | custom-call | tf_op jit(solution)/shard_map/pallas_call | solution.py:388
Async XLA Ops:
  23.6 0.7 %copy-start = (f32[496,128]{1,0:T(8,128)}, f32[496,128]{1,0:T(8,128)S(1)}, u32[]{:S(2)}) copy-start(f32[496,128]{1,0:T(8,128)S(1)} %get-tuple-element.6.vol_ref) | copy-start | bytes 761860
  24.3 0.6 %copy-start.1 = (f32[2,256]{1,0:T(2,128)}, f32[2,256]{1,0:T(2,128)S(1)}, u32[]{:S(2)}) copy-start(f32[2,256]{1,0:T(2,128)S(1)} %get-tuple-element.7.probs_ref) | copy-start | bytes 6148

commit v3 on v2

--- a/solution.py
+++ b/solution.py
@@ -215,7 +215,7 @@
     pad = logs.shape[0]
     lv = logs[...]
     stack = jnp.concatenate(parts(lv, 3) + [jnp.zeros_like(lv)], axis=0).astype(BF16)
-    ll = dot_nt(stack, cnt_b[...])
+    ll = jnp.transpose(dot_nt(cnt_b[...], stack))
     ll = ll[0:pad] + ll[pad : 2 * pad] + ll[2 * pad : 3 * pad]
     scores[...] = (64.0 / pixels) * (ll[0:local] - jnp.concatenate(slice_sums, axis=0))
     each(n - 1, lambda d: score_copy(d).start())
@@ -243,7 +243,8 @@
     arrivals(all_scores, sc_recv, me, n, sc_send)
     top = jnp.max(jnp.max(all_scores[...], axis=0), axis=0, keepdims=True)
     whole_sum = jnp.sum(jnp.sum(jnp.exp(all_scores[...] - top[None]), axis=0), axis=0, keepdims=True)
-    probs_ref[...] = jnp.exp(scores[...] - top) / whole_sum
+
+    own_lane = lax.broadcasted_iota(I32, (GROUP, LANES), 0) == lax.broadcasted_iota(I32, (GROUP, LANES), 1)
 
     def numerators(g):
         pieces = [
@@ -265,11 +266,14 @@
             for i in range(wide):
                 got = lane_pick(num[:, i * LANES : (i + 1) * LANES], lane)
                 acc = jnp.where(row == q * wide + i, got, acc)
-        sums[fr, 0, g] = acc
-        sums[fr, 1, g] = jnp.broadcast_to(den, (GROUP, LANES))
+        sums[fr, g, 0:GROUP] = acc
+        sums[fr, g, GROUP:] = jnp.broadcast_to(
+            jnp.sum(jnp.where(own_lane, den, 0.0), axis=0, keepdims=True), (8, LANES)
+        )
 
     each(total // GROUP, numerators)
     each(m - 1, lambda d: sum_copy(d).start())
+    probs_ref[...] = jnp.exp(scores[...] - top) / whole_sum
 
     def sum_arrivals(d):
         src = lax.rem(fr + d + 1, m)
@@ -282,10 +286,11 @@
     each(m - 1, sum_arrivals)
 
     def scatter(g):
-        num, den = sums[0, 0, g], sums[0, 1, g]
+        both = sums[0, g]
         for f in range(1, m):
-            num = num + sums[f, 0, g]
-            den = den + sums[f, 1, g]
+            both = both + sums[f, g]
+        num = both[0:GROUP]
+        den = jnp.sum(jnp.where(own_lane, both[GROUP : GROUP + 1], 0.0), axis=1, keepdims=True)
         wf = w_mine[g]
         four = parts(num * wf, 2) + parts(den * wf, 2)
         idx = vidx_ref[at(g, GROUP), :]
@@ -372,7 +377,7 @@
             pltpu.VMEM((groups, GROUP, LANES), F32),
             pltpu.VMEM((vox_rows, GROUP * LANES), BF16),
             pltpu.VMEM((4 * LANES, GROUP * LANES), BF16),
-            pltpu.VMEM((m, 2, groups, GROUP, LANES), F32),
+            pltpu.VMEM((m, groups, GROUP + 8, LANES), F32),
             pltpu.VMEM((vox_rows if groups > 1 else 8, 4 * LANES), F32),
             dma((5,)), dma((CHUNKS,)),
             dma((n,)), dma((n,)), dma((n,)), dma((n,)), dma((n,)), dma((n,)),
@@ -394,6 +399,7 @@
         in_specs=[vmem] * 2,
         out_specs=[pl.BlockSpec(memory_space=pl.ANY)] * 2,
         scratch_shapes=[dma((2,))],
+        compiler_params=pltpu.CompilerParams(vmem_limit_bytes=1024 * 1024),
     )(new_volume, probs)
     return (new_volume.reshape(-1), probs)
 

time: 26.8 us -> 24.5 us (0.914)
  local copies, waits for them, and re-layouts: 1.26 us -> 0 us
  Pallas kernels: 24.6 us -> 23.7 us
    unnamed x4 -> x0, local copies, waits for them, and re-layouts: 1.26 us -> none
    pallas_call x1, Pallas kernels: 1.66 us -> 0.72 us  [on_device(): pl.pallas_call(hand_out, out_shape=(jax.ShapeDtypeStruct(new_volume.shape...]
where the time goes in v3:
time: 24.5 us; the launch traced here: 24.3 us
  Pallas kernels  23.7 us (97%)
  between operations  0.64 us (3%)
    pallas_call x1, Pallas kernels, on_device(): pl.pallas_call(functools.partial(kernel, n, m), out_shape=(pltpu.VMEM((vo...  23 us
    pallas_call x1, Pallas kernels, on_device(): pl.pallas_call(hand_out, out_shape=(jax.ShapeDtypeStruct(new_volume.shape...  0.72 us

profile of v3, /device:TPU:0, one launch (start us, length us, event | category | flops | bytes accessed | tf_op | source)
XLA Modules:
  0.0 24.3 jit_solution(1320394994219571039)
XLA Ops:
  0.6 23.0 %shard_map.77 = (f32[496,128]{1,0:T(8,128)S(1)}, f32[2,256]{1,0:T(2,128)S(1)}) custom-call(f32[496,128]{1,0:T(8,128)} %bitcast.3, s32[16,128]{1,0:T(8,128)} %vidx_hbm.1, s32[2,1024]{1,0:T(2,128)} %pix_hbm.1, bf16[2,1024]{1,0:T(2,128)(2,1)} %w_hbm.1, f32[32,128]{1,0:T(8,128)} %bitcast.4, s32[256,4096]{1,0:T(8,128)} %cnt_ref.1), custom_call_target="tpu_custom_call" | custom-call | tf_op jit(solution)/shard_map/pallas_call | solution.py:351
  23.6 0.7 %shard_map.78 = (f32[496,128]{1,0:T(8,128)}, f32[2,256]{1,0:T(2,128)}) custom-call(f32[496,128]{1,0:T(8,128)S(1)} %get-tuple-element.6.vol_ref, f32[2,256]{1,0:T(2,128)S(1)} %get-tuple-element.7.probs_ref), custom_call_target="tpu_custom_call" | custom-call | tf_op jit(solution)/shard_map/pallas_call | solution.py:393

commit v4 on v3

--- a/solution.py
+++ b/solution.py
@@ -215,7 +215,12 @@
     pad = logs.shape[0]
     lv = logs[...]
     stack = jnp.concatenate(parts(lv, 3) + [jnp.zeros_like(lv)], axis=0).astype(BF16)
-    ll = jnp.transpose(dot_nt(cnt_b[...], stack))
+    quarter = pixels // 4
+    ll = [
+        dot_nt(stack[:, q * quarter : (q + 1) * quarter], cnt_b[:, q * quarter : (q + 1) * quarter])
+        for q in range(4)
+    ]
+    ll = (ll[0] + ll[1]) + (ll[2] + ll[3])
     ll = ll[0:pad] + ll[pad : 2 * pad] + ll[2 * pad : 3 * pad]
     scores[...] = (64.0 / pixels) * (ll[0:local] - jnp.concatenate(slice_sums, axis=0))
     each(n - 1, lambda d: score_copy(d).start())
@@ -301,7 +306,10 @@
                 col_val[k * LANES : (k + 1) * LANES, o * LANES : (o + 1) * LANES] = jnp.where(
                     hit, four[k][o : o + 1, :], 0.0
                 ).astype(BF16)
-        return dot_nt(row_hot[...], col_val[...])
+        half = 2 * LANES
+        return jnp.concatenate(
+            [dot_nt(row_hot[...], col_val[0:half]), dot_nt(row_hot[...], col_val[half:])], axis=1
+        )
 
     def finish(acc):
         num = acc[:, 0:LANES] + acc[:, LANES : 2 * LANES]

time: 24.5 us -> 24.5 us (level)
  no operation moved by 1% of the time
where the time goes in v4:
time: 24.5 us; the launch traced here: 24.2 us
  Pallas kernels  23.6 us (96%)
  between operations  0.64 us (3%)
    pallas_call x1, Pallas kernels, on_device(): pl.pallas_call(functools.partial(kernel, n, m), out_shape=(pltpu.VMEM((vo...  22.9 us
    pallas_call x1, Pallas kernels, on_device(): pl.pallas_call(hand_out, out_shape=(jax.ShapeDtypeStruct(new_volume.shape...  0.72 us

profile of v4, /device:TPU:0, one launch (start us, length us, event | category | flops | bytes accessed | tf_op | source)
XLA Modules:
  0.0 24.2 jit_solution(14471056818375201335)
XLA Ops:
  0.6 22.9 %shard_map.77 = (f32[496,128]{1,0:T(8,128)S(1)}, f32[2,256]{1,0:T(2,128)S(1)}) custom-call(f32[496,128]{1,0:T(8,128)} %bitcast.3, s32[16,128]{1,0:T(8,128)} %vidx_hbm.1, s32[2,1024]{1,0:T(2,128)} %pix_hbm.1, bf16[2,1024]{1,0:T(2,128)(2,1)} %w_hbm.1, f32[32,128]{1,0:T(8,128)} %bitcast.4, s32[256,4096]{1,0:T(8,128)} %cnt_ref.1), custom_call_target="tpu_custom_call" | custom-call | tf_op jit(solution)/shard_map/pallas_call | solution.py:359
  23.5 0.7 %shard_map.78 = (f32[496,128]{1,0:T(8,128)}, f32[2,256]{1,0:T(2,128)}) custom-call(f32[496,128]{1,0:T(8,128)S(1)} %get-tuple-element.6.vol_ref, f32[2,256]{1,0:T(2,128)S(1)} %get-tuple-element.7.probs_ref), custom_call_target="tpu_custom_call" | custom-call | tf_op jit(solution)/shard_map/pallas_call | solution.py:401
